TPU v7x, 32 devices: a whole 2x2x4 slice. The times are simulated.
32 devices in a mesh: seq: 4 (over y, core), mem: 8 (over z, x).
Axes of the slice: x: 2, y: 2, z: 4, core: 2. Of those that a mesh axis runs over, the one named last changes fastest.
Arguments:
- queries: bfloat16 [128, 64, 2048], P('mem', 'seq'), may hold values from -40 to 40
- keys: bfloat16 [32, 128, 2048], P('mem'), may hold values from -8 to 8
- values: bfloat16 [32, 128, 2048], P('mem'), may hold values from -6 to 6
- grad_out: bfloat16 [128, 64, 2048], P('mem', 'seq'), may hold values from -6 to 6
- neighbour_owner: int32 [128, 2], replicated, may hold values from 0 to 7, all different within a row; in each aligned block of 16 rows (0 to 15, 16 to 31, ...) at most 6 rows name the same one
- neighbour_row: int32 [128, 2], replicated, may hold values from 0 to 3
Outputs:
- attended: bfloat16 [128, 64, 2048], P('mem', 'seq')
- grad_queries: bfloat16 [128, 64, 2048], P('mem', 'seq')
- grad_keys: bfloat16 [32, 128, 2048], P('mem', 'seq')
- grad_values: bfloat16 [32, 128, 2048], P('mem', 'seq')
Inputs may be any that keep to these rules, and one draw needn't show every extreme that they name: `neighbour_owner`: A group's two entries lie on different shards. Among the 16 groups of one index of mem (aligned blocks of rows) at most 6 name one shard, and exactly 6 do for some shard.
All inputs are finite; a program needn't handle non-finite values.
Results may differ from a plain program's by a relative error of at most 0.015.
Values may be sent and summed in bfloat16 or wider, within the bound.
A program may use at most 128 MiB of HBM per device.

v0:
```python
import math

import jax
import jax.numpy as jnp
from jax import lax
from jax.sharding import PartitionSpec as P

HEADS = 16


def route_tables(owners, shard_cap):
    ref_count = owners.shape[1]
    same_owner = owners[:, :, None] == owners[:, None, :]
    earlier = jnp.arange(ref_count)[None, :] < jnp.arange(ref_count)[:, None]
    rank_table = jnp.sum(same_owner & earlier[None], axis=2)
    return (rank_table, owners * shard_cap + rank_table)


def place_rows(source, slot_table, slot_total):
    buffer = jnp.zeros((slot_total,) + source.shape[1:], source.dtype)
    return buffer.at[slot_table].set(source)


def per_device(queries, keys, values, grad_out, neighbour_owner, neighbour_row):
    senders = lax.axis_size("mem")
    my_index = lax.axis_index("mem")
    group_dev, token_piece, feature_count = queries.shape
    shard_rows, key_len, _ = keys.shape
    head_count = HEADS
    head_width = feature_count // head_count
    scaling = 1.0 / math.sqrt(head_width)
    ref_count = 2 * group_dev
    shard_cap = max(2, 3 * group_dev // senders)
    slot_total = senders * shard_cap
    row_total = slot_total * token_piece
    owners = neighbour_owner.reshape(senders, ref_count)
    row_ids = neighbour_row.reshape(senders, ref_count)
    rank_table, slot_all = route_tables(owners, shard_cap)
    my_slots = lax.dynamic_index_in_dim(slot_all, my_index, 0, keepdims=False)
    owner_hits = owners == my_index
    picked = owner_hits[:, :, None] & (
        rank_table[:, :, None] == jnp.arange(shard_cap)[None, None, :]
    )
    slot_valid = jnp.any(picked, axis=1).reshape(slot_total)
    slot_row = jnp.sum(jnp.where(picked, row_ids[:, :, None], 0), axis=1).reshape(slot_total)
    send_queries = place_rows(jnp.repeat(queries, 2, axis=0), my_slots, slot_total)
    send_grads = place_rows(jnp.repeat(grad_out, 2, axis=0), my_slots, slot_total)
    got_queries = lax.all_to_all(send_queries, "mem", split_axis=0, concat_axis=0, tiled=True)
    query_heads = jnp.moveaxis(got_queries.reshape(row_total, head_count, head_width), 1, 0)
    key_heads = jnp.moveaxis(keys.reshape(shard_rows * key_len, head_count, head_width), 1, 0)
    value_heads = jnp.moveaxis(values.reshape(shard_rows * key_len, head_count, head_width), 1, 0)
    row_owner = jnp.repeat(slot_row, token_piece)
    key_owner = jnp.repeat(jnp.arange(shard_rows, dtype=jnp.int32), key_len)
    own_keys = row_owner[:, None] == key_owner[None, :]

    def head_scores(query_one, key_one):
        return (
            jnp.einsum("td,kd->tk", query_one, key_one, preferred_element_type=jnp.float32)
            * scaling
        )

    def forward_head(operands):
        query_one, key_one, value_one = operands
        scores = head_scores(query_one, key_one)
        peak = jnp.max(jnp.where(own_keys, scores, -jnp.inf), axis=1)
        exponent = jnp.where(own_keys, jnp.exp(scores - peak[:, None]), 0.0).astype(jnp.bfloat16)
        norm = jnp.sum(exponent, axis=1, dtype=jnp.float32)
        mix = (
            jnp.einsum("tk,kd->td", exponent, value_one, preferred_element_type=jnp.float32)
            / norm[:, None]
        )
        return (mix, peak, norm)

    head_mix, row_peak, row_norm = lax.map(forward_head, (query_heads, key_heads, value_heads))
    partial_mix = jnp.moveaxis(head_mix, 0, 1)
    back_mix, back_peak, back_norm = (
        lax.all_to_all(
            partial_mix.reshape(slot_total, token_piece, feature_count),
            "mem",
            split_axis=0,
            concat_axis=0,
            tiled=True,
        ),
        lax.all_to_all(
            row_peak.T.reshape(slot_total, token_piece, head_count),
            "mem",
            split_axis=0,
            concat_axis=0,
            tiled=True,
        ),
        lax.all_to_all(
            row_norm.T.reshape(slot_total, token_piece, head_count),
            "mem",
            split_axis=0,
            concat_axis=0,
            tiled=True,
        ),
    )
    part_mix = jnp.take(back_mix, my_slots, axis=0).reshape(
        group_dev, 2, token_piece, head_count, head_width
    )
    part_peak = jnp.take(back_peak, my_slots, axis=0).reshape(group_dev, 2, token_piece, head_count)
    part_norm = jnp.take(back_norm, my_slots, axis=0).reshape(group_dev, 2, token_piece, head_count)
    row_top = jnp.max(part_peak, axis=1)
    weight = jnp.exp(part_peak - row_top[:, None]) * part_norm
    total_norm = jnp.sum(weight, axis=1)
    attended_heads = (jnp.sum(weight[..., None] * part_mix, axis=1) / total_norm[..., None]).astype(
        jnp.bfloat16
    )
    attended = attended_heads.reshape(group_dev, token_piece, feature_count)
    row_dsum = jnp.sum(
        grad_out.reshape(group_dev, token_piece, head_count, head_width).astype(jnp.float32)
        * attended_heads.astype(jnp.float32),
        axis=3,
    )
    send_top = place_rows(jnp.repeat(row_top, 2, axis=0), my_slots, slot_total)
    send_norm = place_rows(jnp.repeat(total_norm, 2, axis=0), my_slots, slot_total)
    send_dsum = place_rows(jnp.repeat(row_dsum, 2, axis=0), my_slots, slot_total)
    got_grads = lax.all_to_all(send_grads, "mem", split_axis=0, concat_axis=0, tiled=True)
    got_top, got_norm, got_dsum = (
        lax.all_to_all(send_top, "mem", split_axis=0, concat_axis=0, tiled=True),
        lax.all_to_all(send_norm, "mem", split_axis=0, concat_axis=0, tiled=True),
        lax.all_to_all(send_dsum, "mem", split_axis=0, concat_axis=0, tiled=True),
    )
    safe_norm = jnp.where(slot_valid[:, None, None], got_norm, 1.0)
    grad_heads = jnp.moveaxis(got_grads.reshape(row_total, head_count, head_width), 1, 0)
    stat_top = got_top.reshape(row_total, head_count).T
    stat_norm = safe_norm.reshape(row_total, head_count).T
    stat_dsum = got_dsum.reshape(row_total, head_count).T

    def backward_head(operands):
        query_one, key_one, value_one, grad_one, top_one, norm_one, dsum_one = operands
        scores = head_scores(query_one, key_one)
        probability = (
            jnp.where(own_keys, jnp.exp(scores - top_one[:, None]), 0.0) / norm_one[:, None]
        )
        prob_half = probability.astype(jnp.bfloat16)
        value_grad = jnp.einsum(
            "tk,td->kd", prob_half, grad_one, preferred_element_type=jnp.float32
        )
        prob_grad = jnp.einsum("td,kd->tk", grad_one, value_one, preferred_element_type=jnp.float32)
        score_half = (probability * (prob_grad - dsum_one[:, None]) * scaling).astype(jnp.bfloat16)
        query_part = jnp.einsum(
            "tk,kd->td", score_half, key_one, preferred_element_type=jnp.float32
        )
        key_grad = jnp.einsum(
            "tk,td->kd", score_half, query_one, preferred_element_type=jnp.float32
        )
        return (query_part, key_grad, value_grad)

    head_query, head_key, head_value = lax.map(
        backward_head,
        (query_heads, key_heads, value_heads, grad_heads, stat_top, stat_norm, stat_dsum),
    )
    query_parts = jnp.moveaxis(head_query, 0, 1)
    key_grads = jnp.moveaxis(head_key, 0, 1)
    value_grads = jnp.moveaxis(head_value, 0, 1)
    returned = lax.all_to_all(
        query_parts.reshape(slot_total, token_piece, feature_count),
        "mem",
        split_axis=0,
        concat_axis=0,
        tiled=True,
    )
    own_grads = jnp.take(returned, my_slots, axis=0).reshape(
        group_dev, 2, token_piece, feature_count
    )
    grad_queries = (own_grads[:, 0] + own_grads[:, 1]).astype(jnp.bfloat16)
    memory_sums = (
        lax.psum_scatter(
            key_grads.reshape(shard_rows, key_len, feature_count),
            "seq",
            scatter_dimension=1,
            tiled=True,
        ),
        lax.psum_scatter(
            value_grads.reshape(shard_rows, key_len, feature_count),
            "seq",
            scatter_dimension=1,
            tiled=True,
        ),
    )
    return (
        attended,
        grad_queries,
        memory_sums[0].astype(jnp.bfloat16),
        memory_sums[1].astype(jnp.bfloat16),
    )


def solution(mesh):
    placed = (
        P("mem", "seq", None),
        P("mem", None, None),
        P("mem", None, None),
        P("mem", "seq", None),
        P(),
        P(),
    )
    return jax.shard_map(
        per_device,
        mesh=mesh,
        in_specs=placed,
        out_specs=(
            P("mem", "seq", None),
            P("mem", "seq", None),
            P("mem", "seq", None),
            P("mem", "seq", None),
        ),
        check_vma=False,
    )
```

profile of v0, /device:TPU:0, one launch (start us, length us, event | category | flops | bytes accessed | tf_op | source)
XLA Modules:
  0.0 813.9 jit_solution(18318656970991013179)
XLA Ops:
  9.9 2.1 broadcast.68.clone
  12.0 5.4 scatter_fusion
  17.4 7.4 all-to-all-start
  26.1 2.2 copy.58
  32.7 62.8 %all-to-all-done = bf16[48,16,2048]{2,1,0:T(8,128)(2,1)S(1)} async-done(((bf16[48,16,2048]{2,1,0:T(8,128)(2,1)}), bf16[48,16,2048]{2,1,0:T(8,128)(2,1)S(1)}, u32[]{:S(2)}, u32[]{:S(2)}) %all-to-all-start) | async-done | bytes 3145760 | tf_op jit(solution)/shard_map/all_to_all | solution.py:48
  96.5 2.5 copy.35
  99.0 3.3 broadcast.66.clone
  102.3 66.3 %while.30 = (s32[]{:T(128)}, f32[16,768,128]{2,1,0:T(8,128)}, f32[16,768]{1,0:T(8,128)S(1)}, f32[16,768]{1,0:T(8,128)S(1)}, bf16[16,768,128]{2,1,0:T(8,128)(2,1)...) while((s32[]{:T(128)}, f32[16,768,128]{2,1,0:T(8,128)}, ...), condition=%wide.region_6.7_spmd.clone, body=%wide.region_3.0_spmd.clone.sunk | while | flops 206928384 | bytes 5628029 | solution.py:74
  104.4 2.2 fusion.72
  108.5 2.2 fusion.72
  112.6 2.2 fusion.72
  116.8 2.2 fusion.72
  120.9 2.2 fusion.72
  125.1 2.2 fusion.72
  129.2 2.2 fusion.72
  133.4 2.2 fusion.72
  137.5 2.2 fusion.72
  141.6 2.2 fusion.72
  145.8 2.2 fusion.72
  149.9 2.2 fusion.72
  154.0 2.2 fusion.72
  158.1 2.2 fusion.72
  162.3 2.2 fusion.72
  166.4 2.2 fusion.72
  169.6 3.6 all-to-all-start.2
  174.2 5.8 all-to-all-done.2
  180.0 3.3 all-to-all-start.1
  185.7 5.4 scatter_fusion.3
  191.8 6.0 all-to-all-start.6
  201.3 2.2 reduce.6
  211.1 3.0 scatter_fusion.2
  214.9 52.0 %all-to-all-done.6 = bf16[48,16,2048]{2,1,0:T(8,128)(2,1)S(1)} async-done(((bf16[48,16,2048]{2,1,0:T(8,128)(2,1)}), bf16[48,16,2048]{2,1,0:T(8,128)(2,1)S(1)}, u32[]{:S(2)}, u32[]{:S(2)}) %all-to-all-start.6) | async-done | bytes 3145760 | tf_op jit(solution)/shard_map/all_to_all | solution.py:119
  266.9 3.6 all-to-all-start.5
  270.5 9.0 %copy.40 = f32[768,16,128]{2,1,0:T(8,128)} copy(f32[768,16,128]{2,0,1:T(8,128)} %bitcast.163) | data formatting | bytes 12582912 | tf_op jit(solution)/shard_map/transpose | solution.py:75
  279.6 7.1 reshape.183
  287.3 6.0 all-to-all-start.3
  294.2 2.9 copy.62
  299.8 2.8 scatter_fusion.1
  305.9 125.2 %all-to-all-done.3 = f32[48,16,2048]{2,1,0:T(8,128)} async-done(((f32[48,16,2048]{2,1,0:T(8,128)}), f32[48,16,2048]{2,1,0:T(8,128)}, u32[]{:S(2)}, u32[]{:S(2)}) %all-to-all-start.3) | async-done | bytes 6291488 | tf_op jit(solution)/shard_map/all_to_all | solution.py:77
  431.1 4.0 all-to-all-start.4
  435.1 5.7 gather_fusion.2
  440.8 2.7 broadcast_select_fusion.1
  448.6 2.8 scatter_fusion.4
  452.3 5.9 all-to-all-start.7
  460.3 2.2 reduce.8
  466.0 2.2 reduce.10
  469.9 3.3 broadcast.66
  473.2 153.4 %while.31 = (s32[]{:T(128)}, f32[16,768,128]{2,1,0:T(8,128)}, f32[16,512,128]{2,1,0:T(8,128)}, f32[16,512,128]{2,1,0:T(8,128)}, bf16[16,768,128]{2,1,0:T(8,128)(...) while((s32[]{:T(128)}, f32[16,768,128]{2,1,0:T(8,128)}, ...), condition=%wide.region_17.20_spmd.clone, body=%wide.region_16.19_spmd.clone.sunk | while | flops 507248640 | bytes 9214101 | solution.py:151
  574.5 2.1 fusion.84
  593.7 2.1 fusion.84
  626.6 6.6 copy.51
  633.2 4.9 reshape.196
  638.1 9.1 %copy.49 = f32[768,16,128]{2,1,0:T(8,128)} copy(f32[768,16,128]{2,0,1:T(8,128)} %bitcast.162) | data formatting | bytes 12582912 | tf_op jit(solution)/shard_map/transpose | solution.py:155
  647.1 7.4 reshape.193
  654.5 6.0 all-to-all-start.8
  660.8 6.6 copy.50
  667.4 4.9 reshape.195
  674.8 9.1 %reduce-scatter.5.cloned.1.call-done = f32[4,32,2048]{2,1,0:T(8,128)} async-done(((f32[4,128,2048]{2,1,0:T(8,128)}), f32[4,32,2048]{2,1,0:T(8,128)}) %reduce-scatter.5.cloned.1.call-update) | async-done | bytes 1048592 | tf_op jit(solution)/shard_map/reduce_scatter | solution.py:176
  683.9 2.1 convert_element_type.52
  686.0 45.1 %reduce-scatter.3.cloned.1.call-done = f32[4,32,2048]{2,1,0:T(8,128)} async-done(((f32[4,128,2048]{2,1,0:T(8,128)}), f32[4,32,2048]{2,1,0:T(8,128)}) %reduce-scatter.3.cloned.1.call-update) | async-done | bytes 1048592 | tf_op jit(solution)/shard_map/reduce_scatter | solution.py:170
  731.1 2.1 convert_element_type.51
  733.2 64.2 %all-to-all-done.8 = f32[48,16,2048]{2,1,0:T(8,128)} async-done(((f32[48,16,2048]{2,1,0:T(8,128)}), f32[48,16,2048]{2,1,0:T(8,128)}, u32[]{:S(2)}, u32[]{:S(2)}) %all-to-all-start.8) | async-done | bytes 6291488 | tf_op jit(solution)/shard_map/all_to_all | solution.py:158
  797.4 5.8 gather_fusion.3
  803.2 2.7 broadcast_select_fusion
  (313 shorter events, 230.3 us)
Async XLA Ops:
  8.4 177.3 %copy-start.11 = (s32[32]{0:T(128)}, s32[32]{0:T(128)S(1)}, u32[]{:S(2)}) copy-start(s32[32]{0:T(128)S(1)} %fusion.47) | copy-start | bytes 388
  17.4 7.4 copy-start.15
  17.4 78.1 %all-to-all-start = ((bf16[48,16,2048]{2,1,0:T(8,128)(2,1)}), bf16[48,16,2048]{2,1,0:T(8,128)(2,1)S(1)}, u32[]{:S(2)}, u32[]{:S(2)}) async-start(bf16[48,16,2048]{2,1,0:T(8,128)(2,1)} %scatter_fusion), calls=%async_computation | async-start | bytes 6291456 | tf_op jit(solution)/shard_map/all_to_all | solution.py:48
  25.0 0.6 copy-start.13
  28.3 1.9 copy-start.3
  102.3 81.1 %copy-start.1 = (bf16[16,16,2048]{2,1,0:T(8,128)(2,1)S(1)}, bf16[16,16,2048]{2,1,0:T(8,128)(2,1)}, u32[]{:S(2)}) copy-start(bf16[16,16,2048]{2,1,0:T(8,128)(2,1)} %param.17) | copy-start | bytes 3145732
  169.6 10.4 %all-to-all-start.2 = ((f32[8,1,1536]{2,1,0:T(1,128)}), f32[8,1,1536]{2,1,0:T(1,128)S(1)}, u32[]{:S(2)}, u32[]{:S(2)}) async-start(f32[8,1,1536]{2,1,0:T(1,128)} %reshape.285), calls=%async_computation.2 | async-start | bytes 98304 | tf_op jit(solution)/shard_map/all_to_all | solution.py:91
  180.0 11.1 %all-to-all-start.1 = ((f32[8,1,1536]{2,1,0:T(1,128)}), f32[8,1,1536]{2,1,0:T(1,128)S(1)}, u32[]{:S(2)}, u32[]{:S(2)}) async-start(f32[8,1,1536]{2,1,0:T(1,128)} %reshape.287), calls=%async_computation.1 | async-start | bytes 98304 | tf_op jit(solution)/shard_map/all_to_all | solution.py:84
  191.1 0.6 copy-start.10
  191.8 75.1 %all-to-all-start.6 = ((bf16[48,16,2048]{2,1,0:T(8,128)(2,1)}), bf16[48,16,2048]{2,1,0:T(8,128)(2,1)S(1)}, u32[]{:S(2)}, u32[]{:S(2)}) async-start(bf16[48,16,2048]{2,1,0:T(8,128)(2,1)} %scatter_fusion.3), calls=%async_computation.6 | async-start | bytes 6291456 | tf_op jit(solution)/shard_map/all_to_all | solution.py:119
  208.4 2.6 copy-start.6
  210.3 0.8 copy-start.4
  266.9 19.7 %all-to-all-start.5 = ((f32[8,1,1536]{2,1,0:T(1,128)}), f32[8,1,1536]{2,1,0:T(1,128)S(1)}, u32[]{:S(2)}, u32[]{:S(2)}) async-start(f32[8,1,1536]{2,1,0:T(1,128)} %reshape.291), calls=%async_computation.5 | async-start | bytes 98304 | tf_op jit(solution)/shard_map/all_to_all | solution.py:122
  286.6 6.6 copy-start.14
  286.6 0.6 copy-start.9
  287.3 143.8 %all-to-all-start.3 = ((f32[48,16,2048]{2,1,0:T(8,128)}), f32[48,16,2048]{2,1,0:T(8,128)}, u32[]{:S(2)}, u32[]{:S(2)}) async-start(f32[48,16,2048]{2,1,0:T(8,128)} %reshape.183), calls=%async_computation.3 | async-start | bytes 12582912 | tf_op jit(solution)/shard_map/all_to_all | solution.py:77
  298.1 0.9 copy-start.7
  298.1 1.7 copy-start.12
  431.1 21.2 %all-to-all-start.4 = ((f32[8,1,1536]{2,1,0:T(1,128)}), f32[8,1,1536]{2,1,0:T(1,128)}, u32[]{:S(2)}, u32[]{:S(2)}) async-start(f32[8,1,1536]{2,1,0:T(1,128)} %reshape.289), calls=%async_computation.4 | async-start | bytes 98304 | tf_op jit(solution)/shard_map/all_to_all | solution.py:121
  443.5 1.0 copy-start.8
  444.4 1.6 copy-start
  444.4 1.6 copy-start.5
  452.3 13.7 %all-to-all-start.7 = ((f32[8,1,1536]{2,1,0:T(1,128)}), f32[8,1,1536]{2,1,0:T(1,128)}, u32[]{:S(2)}, u32[]{:S(2)}) async-start(f32[8,1,1536]{2,1,0:T(1,128)} %reshape.293), calls=%async_computation.7 | async-start | bytes 98304 | tf_op jit(solution)/shard_map/all_to_all | solution.py:123
  458.2 225.7 %reduce-scatter.5.cloned.1.call-start = ((), (), s32[]{:S(2)}) async-start(), calls=%async_computation.12 | async-start | bytes 5242880 | tf_op jit(solution)/shard_map/reduce_scatter | solution.py:176
  654.5 142.9 %all-to-all-start.8 = ((f32[48,16,2048]{2,1,0:T(8,128)}), f32[48,16,2048]{2,1,0:T(8,128)}, u32[]{:S(2)}, u32[]{:S(2)}) async-start(f32[48,16,2048]{2,1,0:T(8,128)} %reshape.193), calls=%async_computation.8 | async-start | bytes 12582912 | tf_op jit(solution)/shard_map/all_to_all | solution.py:158
  660.5 70.6 %reduce-scatter.3.cloned.1.call-start = ((), (), s32[]{:S(2)}) async-start(), calls=%async_computation.11 | async-start | bytes 5242880 | tf_op jit(solution)/shard_map/reduce_scatter | solution.py:170
  672.3 1.3 copy-start.2
Sparse Core Ops, SparseCore 0:
  638.2 45.6 reduce-scatter.4
  686.6 44.4 reduce-scatter.2
where the time goes:
time: 821 us; the launch traced here: 814 us
  waiting for transfers between devices  364 us (44%)
  matrix products  186 us (23%)
  local copies, waits for them, and re-layouts  168 us (20%)
  starting transfers between devices  46.3 us (6%)
  other arithmetic  34.1 us (4%)
  between operations  14.4 us (2%)
    all_to_all x1, waiting for transfers between devices, per_device(): lax.all_to_all(partial_mix.reshape(slot_total, token_piece, feature_count...  125 us
    all_to_all x1, waiting for transfers between devices, per_device(): lax.all_to_all(query_parts.reshape(slot_total, token_piece, feature_count...  64.2 us
    all_to_all x1, waiting for transfers between devices, per_device(): lax.all_to_all(send_queries, 'mem', split_axis=0, concat_axis=0, tiled=True)  62.8 us
    all_to_all x1, waiting for transfers between devices, per_device(): lax.all_to_all(send_grads, 'mem', split_axis=0, concat_axis=0, tiled=True)  52 us
    dot_general x32, matrix products, head_scores(): jnp.einsum('td,kd->tk', query_one, key_one, preferred_element_type=jnp.fl...  47.2 us
    reduce_scatter x1, waiting for transfers between devices, per_device(): lax.psum_scatter(key_grads.reshape(shard_rows, key_len, feature_count), '...  45.1 us
    dot_general x16, matrix products, forward_head(): jnp.einsum('tk,kd->td', exponent, value_one, preferred_element_type=jnp.f...  35 us
    dot_general x16, matrix products, backward_head(): jnp.einsum('tk,td->kd', score_half, query_one, preferred_element_type=jnp...  32.7 us
  transfers between devices with their start and end apart: 11, of which 7 were waited for; matrix products, arithmetic and copies ran while one was open for 15% of the time, Pallas kernels for 0%

commit v1 on v0

v1 whole, which is shorter than its diff:
```python
import functools
import math

import jax
import jax.numpy as jnp
from jax import lax
from jax.experimental import pallas as pl
from jax.experimental.pallas import tpu as pltpu
from jax.sharding import PartitionSpec as P

HEADS = 16
UNROLL = 4


def matmul(a, b, contract):
    return lax.dot_general(a, b, (contract, ((), ())), preferred_element_type=jnp.float32)


def attention_kernel(scaling, nbr, tokens, memory, outs, grads, sums):
    groups = tokens.shape[1]
    key_len = memory.shape[2]
    sums[...] = jnp.zeros_like(sums)

    def one_group(c, _):
        first, second = nbr[c, 0], nbr[c, 1]
        query, grad = tokens[0, c], tokens[1, c]
        key = jnp.concatenate([memory[first, 0], memory[second, 0]], axis=0)
        value = jnp.concatenate([memory[first, 1], memory[second, 1]], axis=0)
        scores = matmul(query, key, ((1,), (1,))) * scaling
        prob_grad = matmul(grad, value, ((1,), (1,)))
        top = jnp.max(scores, axis=1, keepdims=True)
        exponent = jnp.exp(scores - top)
        norm = jnp.sum(exponent, axis=1, keepdims=True)
        prob = exponent / norm
        prob_half = prob.astype(jnp.bfloat16)
        attended = matmul(prob_half, value, ((1,), (0,))).astype(jnp.bfloat16)
        dsum = jnp.sum(
            grad.astype(jnp.float32) * attended.astype(jnp.float32), axis=1, keepdims=True
        )
        score_half = (prob * (prob_grad - dsum) * scaling).astype(jnp.bfloat16)
        outs[0, c] = attended
        outs[1, c] = matmul(score_half, key, ((1,), (0,))).astype(jnp.bfloat16)
        key_grad = matmul(score_half, query, ((0,), (0,)))
        value_grad = matmul(prob_half, grad, ((0,), (0,)))
        sums[first, 0] += key_grad[:key_len]
        sums[first, 1] += value_grad[:key_len]
        sums[second, 0] += key_grad[key_len:]
        sums[second, 1] += value_grad[key_len:]
        return 0

    lax.fori_loop(0, groups, one_group, 0, unroll=UNROLL)
    grads[...] = sums[...].astype(grads.dtype)


def attention(nbr, tokens, memory, head_width):
    _, groups, group_len, columns = tokens.shape
    entries, _, key_len, _ = memory.shape
    once = pl.Buffered(1) if entries > 64 else None

    def token_spec():
        return pl.BlockSpec((2, groups, group_len, head_width), lambda h, n: (0, 0, 0, h))

    def memory_spec():
        return pl.BlockSpec(
            (entries, 2, key_len, head_width), lambda h, n: (0, 0, 0, h), pipeline_mode=once
        )

    return pl.pallas_call(
        functools.partial(attention_kernel, 1.0 / math.sqrt(head_width)),
        out_shape=(
            jax.ShapeDtypeStruct(tokens.shape, jnp.bfloat16),
            jax.ShapeDtypeStruct(memory.shape, jnp.bfloat16),
        ),
        grid_spec=pltpu.PrefetchScalarGridSpec(
            num_scalar_prefetch=1,
            grid=(columns // head_width,),
            in_specs=[token_spec(), memory_spec()],
            out_specs=[token_spec(), memory_spec()],
            scratch_shapes=[pltpu.VMEM((entries, 2, key_len, head_width), jnp.float32)],
        ),
        compiler_params=pltpu.CompilerParams(vmem_limit_bytes=52 * 2**20),
    )(nbr, tokens, memory)


def per_device(queries, keys, values, grad_out, neighbour_owner, neighbour_row):
    pieces = lax.axis_size("seq")
    group_dev, _, feature_count = queries.shape
    shard_rows = keys.shape[0]
    columns = feature_count // pieces
    head_width = feature_count // HEADS
    start = lax.axis_index("seq") * columns
    nbr_all = (neighbour_owner * shard_rows + neighbour_row).astype(jnp.int32)
    nbr = lax.dynamic_slice_in_dim(nbr_all, lax.axis_index("mem") * group_dev, group_dev, 0)
    own = jnp.stack(
        [
            lax.dynamic_slice_in_dim(keys, start, columns, 2),
            lax.dynamic_slice_in_dim(values, start, columns, 2),
        ],
        axis=1,
    )
    memory = lax.all_gather(own, "mem", axis=0, tiled=True)
    tokens = lax.all_to_all(
        jnp.stack([queries, grad_out]), "seq", split_axis=3, concat_axis=2, tiled=True
    )
    outs, grads = attention(nbr, tokens, memory, head_width)
    grads = lax.psum_scatter(grads, "mem", scatter_dimension=0, tiled=True)
    outs = lax.all_to_all(outs, "seq", split_axis=2, concat_axis=3, tiled=True)
    grads = lax.all_to_all(grads, "seq", split_axis=2, concat_axis=3, tiled=True)
    return (outs[0], outs[1], grads[:, 0], grads[:, 1])


def solution(mesh):
    tokens, whole = P("mem", "seq", None), P("mem", None, None)
    return jax.shard_map(
        per_device,
        mesh=mesh,
        in_specs=(tokens, whole, whole, tokens, P(), P()),
        out_specs=(tokens,) * 4,
        check_vma=False,
    )
```

time: 821 us -> 363 us (0.44)
  matrix products: 186 us -> 0 us
  waiting for transfers between devices: 364 us -> 196 us
  local copies, waits for them, and re-layouts: 168 us -> 91.9 us
  Pallas kernels: 0 us -> 45.8 us
  starting transfers between devices: 46.3 us -> 11.6 us
  other arithmetic: 34.1 us -> 2.48 us
    all_to_all x9 -> x3, waiting for transfers between devices: 310 us -> 34 us  [the longest x1 25.5 us: per_device(): lax.all_to_all(jnp.stack([queries, grad_out]), 'seq', split_axis=3, conca...]
    dot_general x112 -> x0, matrix products: 186 us -> none  [the longest x32 47.2 us: head_scores(): jnp.einsum('td,kd->tk', query_one, key_one, preferred_element_type=jnp.fl...]
    reduce_scatter x2 -> x1, waiting for transfers between devices: 54.2 us -> 140 us  [per_device(): grads = lax.psum_scatter(grads, 'mem', scatter_dimension=0, tiled=True)]
    pallas_call x0 -> x1, Pallas kernels: none -> 45.8 us  [attention(): pl.pallas_call(functools.partial(attention_kernel, 1.0 / math.sqrt(head_w...]
    all_to_all x9 -> x3, starting transfers between devices: 45.8 us -> 11.5 us  [the longest x1 4.38 us: per_device(): lax.all_to_all(jnp.stack([queries, grad_out]), 'seq', split_axis=3, conca...]
    transpose x4 -> x0, local copies, waits for them, and re-layouts: 31.3 us -> none  [the longest x1 9.08 us: per_device(): query_parts = jnp.moveaxis(head_query, 0, 1)]
    reshape x11 -> x0, local copies, waits for them, and re-layouts: 28 us -> none  [the longest x1 7.38 us: per_device(): query_parts.reshape(slot_total, token_piece, feature_count)]
    dynamic_slice x32 -> x1, local copies, waits for them, and re-layouts: 24.6 us -> 0.08 us  [per_device(): lax.dynamic_slice_in_dim(nbr_all, lax.axis_index('mem') * group_dev, grou...]
  transfers between devices with their start and end apart: 11 -> 5, of which waited for: 7 -> 4; matrix products, arithmetic and copies ran while one was open for 15% -> 24% of each run, Pallas kernels for 0% -> 0%
where the time goes in v1:
time: 363 us; the launch traced here: 362 us
  waiting for transfers between devices  196 us (54%)
  local copies, waits for them, and re-layouts  91.9 us (25%)
  Pallas kernels  45.8 us (13%)
  between operations  14.1 us (4%)
  starting transfers between devices  11.6 us (3%)
    reduce_scatter x1, waiting for transfers between devices, per_device(): grads = lax.psum_scatter(grads, 'mem', scatter_dimension=0, tiled=True)  140 us
    pallas_call x1, Pallas kernels, attention(): pl.pallas_call(functools.partial(attention_kernel, 1.0 / math.sqrt(head_w...  45.8 us
    unnamed x13, local copies, waits for them, and re-layouts  36 us
    all_to_all x1, waiting for transfers between devices, per_device(): lax.all_to_all(jnp.stack([queries, grad_out]), 'seq', split_axis=3, conca...  25.5 us
    another operation x1, local copies, waits for them, and re-layouts, per_device(): jnp.stack([queries, grad_out])  23 us
    all_gather x1, waiting for transfers between devices, per_device(): memory = lax.all_gather(own, 'mem', axis=0, tiled=True)  22.8 us
    all_to_all x1, local copies, waits for them, and re-layouts, per_device(): lax.all_to_all(jnp.stack([queries, grad_out]), 'seq', split_axis=3, conca...  17.1 us
    all_to_all x1, waiting for transfers between devices, per_device(): lax.all_to_all(grads, 'seq', split_axis=2, concat_axis=3, tiled=True)  8.45 us
  transfers between devices with their start and end apart: 5, of which 4 were waited for; matrix products, arithmetic and copies ran while one was open for 24% of the time, Pallas kernels for 0%

profile of v1, /device:TPU:0, one launch (start us, length us, event | category | flops | bytes accessed | tf_op | source)
XLA Modules:
  0.0 362.3 jit_solution(12797141886067469232)
XLA Ops:
  7.2 0.0 all-gather.2.cloned.1.call-start
  7.2 1.3 dynamic-slice_bitcast_fusion
  8.5 0.0 copy-start.2
  8.5 1.1 pad_maximum_fusion.1
  9.6 0.0 all-gather.2.cloned.1.call-update
  9.6 0.5 copy-done.2
  10.1 1.4 pad_maximum_fusion
  11.6 23.0 %copy.39 = bf16[2,16,16,2048]{2,1,0,3:T(8,128)(2,1)} copy(bf16[2,16,16,2048]{3,2,1,0:T(8,128)(2,1)S(1)} %pad_maximum_fusion) | data formatting | bytes 4194304 | tf_op jit(solution)/shard_map/stack | solution.py:103
  34.5 20.4 %reshape.12 = bf16[4,2,131072]{2,1,0:T(2,128)(2,1)} reshape(bf16[2048,2,16,16]{3,2,1,0:T(8,128)(2,1)} %bitcast.24) | data formatting | bytes 4194304
  54.9 0.0 copy-start.3
  54.9 0.0 copy-start.4
  54.9 4.4 %all-to-all-start = ((bf16[4,2,131072]{2,1,0:T(2,128)(2,1)}), bf16[4,2,131072]{2,1,0:T(2,128)(2,1)S(1)}, u32[]{:S(2)}, u32[]{:S(2)}) async-start(bf16[4,2,131072]{2,1,0:T(2,128)(2,1)} %reshape.12), calls=%async_computation | async-start | bytes 4194304 | tf_op jit(solution)/shard_map/all_to_all | solution.py:102
  59.3 0.0 reduce-scatter.2.cloned.1.call-start
  59.3 0.0 copy-done.3
  59.3 0.0 copy-done.4
  59.3 0.1 constant_dynamic-slice_fusion
  59.4 0.1 copy.46.nbr
  59.5 25.5 %all-to-all-done = bf16[4,2,131072]{2,1,0:T(2,128)(2,1)S(1)} async-done(((bf16[4,2,131072]{2,1,0:T(2,128)(2,1)}), bf16[4,2,131072]{2,1,0:T(2,128)(2,1)S(1)}, u32[]{:S(2)}, u32[]{:S(2)}) %all-to-all-start) | async-done | bytes 2097184 | tf_op jit(solution)/shard_map/all_to_all | solution.py:102
  85.0 13.4 %reshape.13 = bf16[2048,2,16,16]{3,2,1,0:T(8,128)(2,1)} reshape(bf16[4,2,131072]{2,1,0:T(2,128)(2,1)S(1)} %all-to-all-done) | data formatting | bytes 4194304
  98.4 17.1 %copy.40 = bf16[2,16,16,4,512]{4,2,3,1,0:T(8,128)(2,1)} copy(bf16[2,16,16,4,512]{2,1,0,4,3:T(8,128)(2,1)} %bitcast.25) | data formatting | bytes 4194304 | tf_op jit(solution)/shard_map/all_to_all | solution.py:102
  115.6 22.8 %all-gather.2.cloned.1.call-done.memory = bf16[32,2,128,512]{3,2,1,0:T(8,128)(2,1)} async-done(((bf16[4,2,128,512]{3,2,1,0:T(8,128)(2,1)}), bf16[32,2,128,512]{3,2,1,0:T(8,128)(2,1)}) %all-gather.2.cloned.1.call-update) | async-done | bytes 8388624 | tf_op jit(solution)/shard_map/all_gather | solution.py:101
  138.4 45.8 %shard_map.93 = (bf16[2,16,64,512]{3,2,1,0:T(8,128)(2,1)}, bf16[32,2,128,512]{3,2,1,0:T(8,128)(2,1)}) custom-call(s32[16,2]{1,0:T(8,128)S(1)} %copy.46.nbr, bf16[2,16,64,512]{3,2,1,0:T(8,128)(2,1)} %bitcast.27, bf16[32,2,128,512]{3,2,1,0:T(8,128)(2,1)} %all-gather.2.cloned.1.call-done.memory), custom_call_target="tpu_custom_call" | custom-call | tf_op jit(solution)/shard_map/pallas_call | solution.py:68
  184.2 0.0 copy-start.1
  184.2 0.0 reduce-scatter.2.cloned.1.call-update
  184.2 1.6 copy-done.1
  185.8 2.6 copy.41
  188.3 3.6 all-to-all-start.1
  191.9 139.6 %reduce-scatter.2.cloned.1.call-done = bf16[4,2,128,512]{3,2,1,0:T(8,128)(2,1)} async-done(((bf16[32,2,128,512]{3,2,1,0:T(8,128)(2,1)}), bf16[4,2,128,512]{3,2,1,0:T(8,128)(2,1)}) %reduce-scatter.2.cloned.1.call-update) | async-done | bytes 1048592 | tf_op jit(solution)/shard_map/reduce_scatter | solution.py:106
  331.5 3.3 copy.44
  334.8 0.0 all-to-all-done.1
  334.8 3.5 all-to-all-start.2
  338.4 1.2 fusion
  339.5 0.0 copy-start
  339.5 0.8 copy.42
  340.3 1.6 squeeze.12
  341.9 0.0 copy-done
  341.9 0.8 copy.43
  342.7 1.6 squeeze.13
  344.3 8.5 %all-to-all-done.2 = bf16[4,2,128,512]{3,1,0,2:T(2,128)(2,1)S(1)} async-done(((bf16[4,2,128,512]{3,1,0,2:T(2,128)(2,1)}), bf16[4,2,128,512]{3,1,0,2:T(2,128)(2,1)S(1)}, u32[]{:S(2)}, u32[]{:S(2)}) %all-to-all-start.2) | async-done | bytes 1048608 | tf_op jit(solution)/shard_map/all_to_all | solution.py:108
  352.8 0.8 copy.45
  353.6 0.8 all_to_all.47
  354.4 1.0 slice_bitcast_fusion
  (1 shorter events, 0.0 us)
Async XLA Ops:
  7.2 131.2 %all-gather.2.cloned.1.call-start = ((), (), s32[]{:S(2)}) async-start(), calls=%async_computation.4 | async-start | bytes 9437184 | tf_op jit(solution)/shard_map/all_gather | solution.py:101
  8.5 1.6 copy-start.2
  54.9 4.4 %copy-start.3 = (s32[128,2]{0,1:T(2,128)S(1)}, s32[128,2]{0,1:T(2,128)}, u32[]{:S(2)}) copy-start(s32[128,2]{0,1:T(2,128)} %param.11) | copy-start | bytes 3076
  54.9 4.4 %copy-start.4 = (s32[128,2]{0,1:T(2,128)S(1)}, s32[128,2]{0,1:T(2,128)}, u32[]{:S(2)}) copy-start(s32[128,2]{0,1:T(2,128)} %param.10) | copy-start | bytes 3076
  54.9 30.1 %all-to-all-start = ((bf16[4,2,131072]{2,1,0:T(2,128)(2,1)}), bf16[4,2,131072]{2,1,0:T(2,128)(2,1)S(1)}, u32[]{:S(2)}, u32[]{:S(2)}) async-start(bf16[4,2,131072]{2,1,0:T(2,128)(2,1)} %reshape.12), calls=%async_computation | async-start | bytes 4194304 | tf_op jit(solution)/shard_map/all_to_all | solution.py:102
  59.3 272.2 %reduce-scatter.2.cloned.1.call-start = ((), (), s32[]{:S(2)}) async-start(), calls=%async_computation.5 | async-start | bytes 9437184 | tf_op jit(solution)/shard_map/reduce_scatter | solution.py:106
  184.2 1.6 copy-start.1
  188.3 146.5 %all-to-all-start.1 = ((bf16[2,16,64,512]{3,1,0,2:T(8,128)(2,1)}), bf16[2,16,64,512]{3,1,0,2:T(8,128)(2,1)S(1)}, u32[]{:S(2)}, u32[]{:S(2)}) async-start(bf16[2,16,64,512]{3,1,0,2:T(8,128)(2,1)} %copy.41), calls=%async_computation.1 | async-start | bytes 4194304 | tf_op jit(solution)/shard_map/all_to_all | solution.py:107
  334.8 18.0 %all-to-all-start.2 = ((bf16[4,2,128,512]{3,1,0,2:T(2,128)(2,1)}), bf16[4,2,128,512]{3,1,0,2:T(2,128)(2,1)S(1)}, u32[]{:S(2)}, u32[]{:S(2)}) async-start(bf16[4,2,128,512]{3,1,0,2:T(2,128)(2,1)} %copy.44), calls=%async_computation.3 | async-start | bytes 2097152 | tf_op jit(solution)/shard_map/all_to_all | solution.py:108
  339.5 2.4 copy-start
Sparse Core Ops, SparseCore 0:
  10.7 127.6 all-gather.1
  184.3 147.1 reduce-scatter.1
